TPU v7x, 512 devices: a whole 4x4x16 slice. The times are simulated.
512 devices in a mesh: grid: 128 (over x, y_hi, z), freq: 4 (over y_lo, core).
Axes of the slice: x: 4, y: 4 (y_hi: 2, y_lo: 2; y = y_hi * 2 + y_lo), z: 16, core: 2. Of those that a mesh axis runs over, the one named last changes fastest.
Arguments:
- amplitude: bfloat16 [16384, 2048], P('grid', 'freq'), may hold values from 0.5 to 1.5
- spectrum: float32 [2048], P('freq'), may hold values from 0.3 to 3
- freq_index: int32 [2, 2048], P(None, 'freq'), may hold values from -128 to 128
- star_offsets: int32 [9, 2], replicated, may hold values from -8 to 8
- valid_mask: int32 [16384], P('grid'), may hold values 0 or 1
Outputs:
- covariance: bfloat16 [128, 2048, 1024], P('grid', 'freq')
All inputs are finite; a program needn't handle non-finite values. No bound on the sum of `valid_mask` on one device may be relied on, other than what follows from the above.
Results may differ from a plain program's by a relative error of at most 0.013.
Values may be sent and summed in bfloat16 or wider, within the bound.
A program may use at most 64 MiB of HBM per device.

v0:
```python
import math

import jax
import jax.numpy as jnp
from jax import lax
from jax.sharding import PartitionSpec as P

NGS = 9
SIDE = 64


def swapped(array, axis, distance):
    return lax.ppermute(array, axis, [(i, i ^ 1 << distance) for i in range(lax.axis_size(axis))])


def local_operand(amplitude, spectrum, freq_index, star_offsets, valid_mask):
    panel_rows = amplitude.shape[0]
    slope_count = panel_rows * lax.axis_size("grid")
    freq_total = amplitude.shape[1] * lax.axis_size("freq")
    slope_index = lax.axis_index("grid") * panel_rows + jnp.arange(panel_rows, dtype=jnp.int32)
    star_index = slope_index * NGS // slope_count
    subaperture = slope_index // 2
    across = subaperture % SIDE
    upward = subaperture // SIDE % SIDE
    selector = (star_index[:, None] == jnp.arange(NGS, dtype=jnp.int32)[None, :]).astype(jnp.int32)
    shift_x = jnp.sum(selector * star_offsets[None, :, 0], axis=1)
    shift_y = jnp.sum(selector * star_offsets[None, :, 1], axis=1)
    phase_index = jnp.mod(
        freq_index[0][None, :] * (2 * across + shift_x)[:, None]
        + freq_index[1][None, :] * (2 * upward + shift_y)[:, None],
        512,
    )
    angles = phase_index.astype(jnp.float32) * (2.0 * math.pi / 512.0)
    scaling = (
        valid_mask.astype(jnp.float32)[:, None]
        * amplitude.astype(jnp.float32)
        * jnp.sqrt(spectrum / freq_total)[None, :]
    )
    return jnp.concatenate([scaling * jnp.cos(angles), scaling * jnp.sin(angles)], axis=1).astype(
        jnp.bfloat16
    )


def arrange(gathered, partner, which_bit, grid_index):
    is_lower = grid_index // 2**which_bit % 2 == 0
    return jnp.where(
        is_lower, jnp.concatenate([gathered, partner], 0), jnp.concatenate([partner, gathered], 0)
    )


def row_step(gathered, which_bit, grid_index):
    partner = swapped(gathered, "grid", which_bit)
    return arrange(gathered, partner, which_bit, grid_index)


def column_step(gathered, which_bit, grid_index):
    partner = swapped(gathered, "grid", which_bit)
    return arrange(gathered, partner, which_bit, grid_index)


def on_device(amplitude, spectrum, freq_index, star_offsets, valid_mask):
    operand = local_operand(amplitude, spectrum, freq_index, star_offsets, valid_mask)
    levels = lax.axis_size("grid").bit_length() - 1
    row_levels = min(4, levels - 1)
    grid_index = lax.axis_index("grid")
    row_digits = list(range(row_levels))
    column_digits = list(range(row_levels, levels))
    row_block = operand
    column_block = operand
    for which_bit in row_digits:
        row_block = row_step(row_block, which_bit, grid_index)
    for which_bit in column_digits:
        column_block = column_step(column_block, which_bit, grid_index)
    summed = lax.psum_scatter(
        lax.dot_general(
            row_block, column_block, (((1,), (1,)), ((), ())), preferred_element_type=jnp.float32
        ).astype(jnp.bfloat16),
        "freq",
        scatter_dimension=0,
        tiled=True,
    )
    return summed[None]


def solution(mesh):
    placed = (P("grid", "freq"), P("freq"), P(None, "freq"), P(), P("grid"))
    return jax.shard_map(
        on_device, mesh=mesh, in_specs=placed, out_specs=P("grid", "freq", None), check_vma=False
    )
```

profile of v0, /device:TPU:1, one launch (start us, length us, event | category | flops | bytes accessed | tf_op | source)
XLA Modules:
  0.0 459.1 jit_solution(9967195474348977790)
XLA Ops:
  6.5 0.7 convert_element_type.14
  7.2 0.8 slice_bitcast_fusion
  8.0 0.7 multiply_sqrt_fusion
  8.7 0.8 fusion.23
  9.5 2.2 multiply_convert_fusion.1
  11.7 5.7 %collective-permute-start.4 = (bf16[128,1024]{1,0:T(8,128)(2,1)S(1)}, bf16[128,1024]{1,0:T(8,128)(2,1)S(1)}, u32[]{:S(2)}, u32[]{:S(2)}) collective-permute-start(bf16[128,1024]{1,0:T(8,128)(2,1)S(1)} %pad_maximum_fusion.2), channel_id=1, source_target_pairs={{0,64},{4,68},{8,72},{12,76},{16,80},{20,84},{24,88},{28,92},{32,9... | collective-permute-start | bytes 786440 | tf_op jit(solution)/shard_map/ppermute | solution.py:13
  17.4 3.5 collective-permute-start
  21.1 4.1 collective-permute-done
  25.3 0.3 maximum_select_fusion.10
  25.6 6.2 %collective-permute-start.1 = (bf16[256,1024]{1,0:T(8,128)(2,1)S(1)}, bf16[256,1024]{1,0:T(8,128)(2,1)S(1)}, u32[]{:S(2)}, u32[]{:S(2)}) collective-permute-start(bf16[256,1024]{1,0:T(8,128)(2,1)S(1)} %get-tuple-element.8), channel_id=1, source_target_pairs={{0,8},{4,12},{8,0},{12,4},{16,24},{20,28},{24,16},{28,20},{32,40},... | collective-permute-start | bytes 1572872 | tf_op jit(solution)/shard_map/ppermute | solution.py:13
  31.8 22.5 %collective-permute-done.1 = bf16[256,1024]{1,0:T(8,128)(2,1)S(1)} collective-permute-done((bf16[256,1024]{1,0:T(8,128)(2,1)S(1)}, bf16[256,1024]{1,0:T(8,128)(2,1)S(1)}, u32[]{:S(2)}, u32[]{:S(2)}) %collective-permute-start.1) | collective-permute-done | bytes 524320 | tf_op jit(solution)/shard_map/ppermute | solution.py:13
  54.4 0.5 maximum_select_fusion.7
  54.9 8.8 %collective-permute-start.2 = (bf16[512,1024]{1,0:T(8,128)(2,1)S(1)}, bf16[512,1024]{1,0:T(8,128)(2,1)S(1)}, u32[]{:S(2)}, u32[]{:S(2)}) collective-permute-start(bf16[512,1024]{1,0:T(8,128)(2,1)S(1)} %maximum_select_fusion.7), channel_id=1, source_target_pairs={{0,16},{4,20},{8,24},{12,28},{16,0},{20,4},{24,8},{28,12},{32,48},... | collective-permute-start | bytes 3145736 | tf_op jit(solution)/shard_map/ppermute | solution.py:13
  63.7 135.2 %collective-permute-done.2 = bf16[512,1024]{1,0:T(8,128)(2,1)S(1)} collective-permute-done((bf16[512,1024]{1,0:T(8,128)(2,1)S(1)}, bf16[512,1024]{1,0:T(8,128)(2,1)S(1)}, u32[]{:S(2)}, u32[]{:S(2)}) %collective-permute-start.2) | collective-permute-done | bytes 1048608 | tf_op jit(solution)/shard_map/ppermute | solution.py:13
  198.9 2.3 maximum_select_fusion.4
  201.2 103.0 %collective-permute-start.3 = (bf16[1024,1024]{1,0:T(8,128)(2,1)}, bf16[1024,1024]{1,0:T(8,128)(2,1)}, u32[]{:S(2)}, u32[]{:S(2)}) collective-permute-start(bf16[1024,1024]{1,0:T(8,128)(2,1)} %maximum_select_fusion.4), channel_id=1, source_target_pairs={{0,32},{4,36},{8,40},{12,44},{16,48},{20,52},{24,56},{28,60},{32,0... | collective-permute-start | bytes 6291464 | tf_op jit(solution)/shard_map/ppermute | solution.py:13
  304.2 3.1 collective-permute-start.5
  307.4 11.5 %collective-permute-done.5 = bf16[256,1024]{1,0:T(8,128)(2,1)S(1)} collective-permute-done((bf16[256,1024]{1,0:T(8,128)(2,1)S(1)}, bf16[256,1024]{1,0:T(8,128)(2,1)S(1)}, u32[]{:S(2)}, u32[]{:S(2)}) %collective-permute-start.5) | collective-permute-done | bytes 524320 | tf_op jit(solution)/shard_map/ppermute | solution.py:13
  318.9 0.5 maximum_select_fusion.8
  319.3 4.7 %collective-permute-start.6 = (bf16[512,1024]{1,0:T(8,128)(2,1)S(1)}, bf16[512,1024]{1,0:T(8,128)(2,1)S(1)}, u32[]{:S(2)}, u32[]{:S(2)}) collective-permute-start(bf16[512,1024]{1,0:T(8,128)(2,1)S(1)} %maximum_select_fusion.8), channel_id=1, source_target_pairs={{0,256},{4,260},{8,264},{12,268},{16,272},{20,276},{24,280},{28,28... | collective-permute-start | bytes 3145736 | tf_op jit(solution)/shard_map/ppermute | solution.py:13
  324.1 21.8 %collective-permute-done.6 = bf16[512,1024]{1,0:T(8,128)(2,1)S(1)} collective-permute-done((bf16[512,1024]{1,0:T(8,128)(2,1)S(1)}, bf16[512,1024]{1,0:T(8,128)(2,1)S(1)}, u32[]{:S(2)}, u32[]{:S(2)}) %collective-permute-start.6) | collective-permute-done | bytes 1048608 | tf_op jit(solution)/shard_map/ppermute | solution.py:13
  345.9 49.2 %collective-permute-done.3 = bf16[1024,1024]{1,0:T(8,128)(2,1)} collective-permute-done((bf16[1024,1024]{1,0:T(8,128)(2,1)}, bf16[1024,1024]{1,0:T(8,128)(2,1)}, u32[]{:S(2)}, u32[]{:S(2)}) %collective-permute-start.3) | collective-permute-done | bytes 2097184 | tf_op jit(solution)/shard_map/ppermute | solution.py:13
  395.1 10.1 %fusion.7 = bf16[2048,1024]{1,0:T(8,128)(2,1)} fusion(bf16[1024,1024]{1,0:T(8,128)(2,1)} %collective-permute-done.3, bf16[1024,1024]{1,0:T(8,128)(2,1)} %maximum_select_fusion.4, pred[]{:T(512)S(6)} %eq.47, bf16[512,1024]{1,0:T(8,128)(2,1)S(1)} %collective-permute-done.6, bf16[512,1024]{1,0:T(8,128)(2,1)S(1)} %maximum_select_fusion.8, pred[]{:T(512)S(6)} %eq.54), kind=kOutput, calls=%fused_computation.8 | convolution fusion | flops 4325376000 | bytes 10485762 | tf_op jit(solution)/shard_map/dot_general | solution.py:75
  405.2 47.0 %reduce-scatter.2.cloned.1.call-done = bf16[512,1024]{1,0:T(8,128)(2,1)} async-done(((bf16[2048,1024]{1,0:T(8,128)(2,1)}), bf16[512,1024]{1,0:T(8,128)(2,1)}) %reduce-scatter.2.cloned.1.call-update) | async-done | bytes 1048592 | tf_op jit(solution)/shard_map/reduce_scatter | solution.py:74
  (7 shorter events, 0.3 us)
Async XLA Ops:
  6.5 445.7 %reduce-scatter.2.cloned.1.call-start = ((), (), s32[]{:S(2)}) async-start(), calls=%async_computation.1 | async-start | bytes 5242880 | tf_op jit(solution)/shard_map/reduce_scatter | solution.py:74
  11.7 9.4 %collective-permute-start.4 = (bf16[128,1024]{1,0:T(8,128)(2,1)S(1)}, bf16[128,1024]{1,0:T(8,128)(2,1)S(1)}, u32[]{:S(2)}, u32[]{:S(2)}) collective-permute-start(bf16[128,1024]{1,0:T(8,128)(2,1)S(1)} %pad_maximum_fusion.2), channel_id=1, source_target_pairs={{0,64},{4,68},{8,72},{12,76},{16,80},{20,84},{24,88},{28,92},{32,9... | collective-permute-start | bytes 786440 | tf_op jit(solution)/shard_map/ppermute | solution.py:13
  17.4 7.9 %collective-permute-start = (bf16[128,1024]{1,0:T(8,128)(2,1)S(1)}, bf16[128,1024]{1,0:T(8,128)(2,1)S(1)}, u32[]{:S(2)}, u32[]{:S(2)}) collective-permute-start(bf16[128,1024]{1,0:T(8,128)(2,1)S(1)} %pad_maximum_fusion.2), channel_id=1, source_target_pairs={{0,4},{4,0},{8,12},{12,8},{16,20},{20,16},{24,28},{28,24},{32,36},... | collective-permute-start | bytes 786440 | tf_op jit(solution)/shard_map/ppermute | solution.py:13
  25.6 28.7 %collective-permute-start.1 = (bf16[256,1024]{1,0:T(8,128)(2,1)S(1)}, bf16[256,1024]{1,0:T(8,128)(2,1)S(1)}, u32[]{:S(2)}, u32[]{:S(2)}) collective-permute-start(bf16[256,1024]{1,0:T(8,128)(2,1)S(1)} %get-tuple-element.8), channel_id=1, source_target_pairs={{0,8},{4,12},{8,0},{12,4},{16,24},{20,28},{24,16},{28,20},{32,40},... | collective-permute-start | bytes 1572872 | tf_op jit(solution)/shard_map/ppermute | solution.py:13
  54.9 144.0 %collective-permute-start.2 = (bf16[512,1024]{1,0:T(8,128)(2,1)S(1)}, bf16[512,1024]{1,0:T(8,128)(2,1)S(1)}, u32[]{:S(2)}, u32[]{:S(2)}) collective-permute-start(bf16[512,1024]{1,0:T(8,128)(2,1)S(1)} %maximum_select_fusion.7), channel_id=1, source_target_pairs={{0,16},{4,20},{8,24},{12,28},{16,0},{20,4},{24,8},{28,12},{32,48},... | collective-permute-start | bytes 3145736 | tf_op jit(solution)/shard_map/ppermute | solution.py:13
  201.2 193.9 %collective-permute-start.3 = (bf16[1024,1024]{1,0:T(8,128)(2,1)}, bf16[1024,1024]{1,0:T(8,128)(2,1)}, u32[]{:S(2)}, u32[]{:S(2)}) collective-permute-start(bf16[1024,1024]{1,0:T(8,128)(2,1)} %maximum_select_fusion.4), channel_id=1, source_target_pairs={{0,32},{4,36},{8,40},{12,44},{16,48},{20,52},{24,56},{28,60},{32,0... | collective-permute-start | bytes 6291464 | tf_op jit(solution)/shard_map/ppermute | solution.py:13
  304.2 14.6 %collective-permute-start.5 = (bf16[256,1024]{1,0:T(8,128)(2,1)S(1)}, bf16[256,1024]{1,0:T(8,128)(2,1)S(1)}, u32[]{:S(2)}, u32[]{:S(2)}) collective-permute-start(bf16[256,1024]{1,0:T(8,128)(2,1)S(1)} %get-tuple-element.7), channel_id=1, source_target_pairs={{0,128},{4,132},{8,136},{12,140},{16,144},{20,148},{24,152},{28,15... | collective-permute-start | bytes 1572872 | tf_op jit(solution)/shard_map/ppermute | solution.py:13
  319.3 26.5 %collective-permute-start.6 = (bf16[512,1024]{1,0:T(8,128)(2,1)S(1)}, bf16[512,1024]{1,0:T(8,128)(2,1)S(1)}, u32[]{:S(2)}, u32[]{:S(2)}) collective-permute-start(bf16[512,1024]{1,0:T(8,128)(2,1)S(1)} %maximum_select_fusion.8), channel_id=1, source_target_pairs={{0,256},{4,260},{8,264},{12,268},{16,272},{20,276},{24,280},{28,28... | collective-permute-start | bytes 3145736 | tf_op jit(solution)/shard_map/ppermute | solution.py:13
Sparse Core Ops, SparseCore 0:
  405.3 46.8 reduce-scatter.1
where the time goes:
time: 459 us
  waiting for transfers between devices  292 us (64%)
  starting transfers between devices  135 us (29%)
  between operations  13.7 us (3%)
  matrix products  10.1 us (2%)
  other arithmetic  7.28 us (2%)
    ppermute x7, waiting for transfers between devices, swapped(): lax.ppermute(array, axis, [(i, i ^ 1 << distance) for i in range(lax.axis...  245 us
    ppermute x7, starting transfers between devices, swapped(): lax.ppermute(array, axis, [(i, i ^ 1 << distance) for i in range(lax.axis...  135 us
    reduce_scatter x1, waiting for transfers between devices, on_device(): lax.psum_scatter(lax.dot_general(row_block, column_block, (((1,), (1,)),...  47 us
    dot_general x1, matrix products, on_device(): lax.dot_general(row_block, column_block, (((1,), (1,)), ((), ())), prefer...  10.1 us
  transfers between devices with their start and end apart: 8, of which 8 were waited for; matrix products, arithmetic and copies ran while one was open for 0% of the time, Pallas kernels for 0%

commit v1 on v0

v1 whole, which is shorter than its diff:
```python
import math

import jax
import jax.numpy as jnp
from jax import lax
from jax.experimental import pallas as pl
from jax.experimental.pallas import tpu as pltpu
from jax.sharding import PartitionSpec as P

NGS = 9
PANEL = 128
NZ = 16
NX = 4
SUBS = 4
HALF = NZ // 2
MESH = pl.DeviceIdType.MESH


def cos_sin(phase):
    index = phase.astype(jnp.int32) & 511
    quadrant = (index + 64) >> 7
    x = (index - (quadrant << 7)).astype(jnp.float32) * (2.0 * math.pi / 512.0)
    y = x * x
    sin = x * (1.0 + y * (-1 / 6 + y * (1 / 120 + y * (-1 / 5040 + y * (1 / 362880)))))
    cos = 1.0 + y * (-0.5 + y * (1 / 24 + y * (-1 / 720 + y * (1 / 40320 + y * (-1 / 3628800)))))
    swap = (quadrant & 1) == 1
    cos, sin = jnp.where(swap, sin, cos), jnp.where(swap, cos, sin)
    cos = jnp.where(((quadrant + 1) & 2) != 0, -cos, cos)
    sin = jnp.where((quadrant & 2) != 0, -sin, sin)
    return cos, sin


def kernel(
    amp_ref, spec_ref, freq_ref, star_ref, mask_ref, out_ref,
    rows, cols, rop, cop, pack, base_c, base_s, turn_p, turn_c, turn_s, mask_t, acc,
    zs, zr, hs, hr, ps, pr, ys, yr, xs, xr, fs, fr, ss, sr,
):
    g, f = lax.axis_index("grid"), lax.axis_index("freq")
    z, a = g % NZ, g // NZ
    x, yh = a // 2, a % 2
    yl, core = f // 2, f % 2
    width = amp_ref.shape[1]

    f1 = f + 1 - 2 * core
    f2 = f + 2 - 4 * yl
    f3 = f1 + 2 - 4 * yl
    a_far = a + 1 - 2 * yh
    g_far = a_far * NZ + z

    def at_z(step):
        return a * NZ + (z + step + NZ) % NZ

    def at_x(step):
        return (((x + step + NX) % NX) * 2 + yh) * NZ + z

    barrier = pltpu.get_barrier_semaphore()
    peers = [
        (at_z(1), f), (at_z(-1), f), (g, f1), (g, f2), (g, f3),
        (g_far, f), (g_far, f2), (at_x(1), f), (at_x(-1), f),
    ]
    for peer in peers:
        pl.semaphore_signal(barrier, inc=1, device_id=peer, device_id_type=MESH)

    mask_t[...] = jnp.broadcast_to(mask_ref[...].astype(jnp.float32), (PANEL, PANEL)).T
    for n in range(width // 128):
        lanes = pl.ds(n * 128, 128)
        masked = (amp_ref[:, lanes].astype(jnp.float32) * mask_t[...]).astype(jnp.bfloat16)
        rows[z, f, :, lanes] = masked
        cols[f, a, :, lanes] = masked
    total = width * lax.axis_size("freq")
    pack[f, 0:2, :] = freq_ref[...].astype(jnp.float32)
    pack[f, 2:3, :] = jnp.sqrt(spec_ref[...] / total)

    pl.semaphore_wait(barrier, len(peers))

    started = []

    def send(src, dst, send_sem, recv_sem, peer):
        return pltpu.make_async_remote_copy(
            src_ref=src, dst_ref=dst, send_sem=send_sem, recv_sem=recv_sem,
            device_id=peer, device_id_type=MESH,
        )

    def begin(copy):
        copy.start()
        started.append(copy)

    piece = PANEL // SUBS

    def ring(t, way, sub):
        panel = (z - (1, -1)[way] * (t - 1) + NZ) % NZ
        part = rows.at[panel, f, pl.ds(sub * piece, piece)]
        return send(part, part, zs.at[way, t - 1, sub], zr.at[way, t - 1, sub], (at_z((1, -1)[way]), f))

    def ring_got(t, way, sub):
        panel = (z - (1, -1)[way] * t + NZ) % NZ
        part = rows.at[panel, f, pl.ds(sub * piece, piece)]
        send(part, part, zs.at[way, t - 1, sub], zr.at[way, t - 1, sub], (at_z((1, -1)[way]), f)).wait_recv()

    def ways(t, sub):
        if t < HALF:
            return (0, 1)
        return (0,) if sub < SUBS // 2 else (1,)

    def hand(slot, panel, start):
        owner, place = panel // 4, panel % 4

        @pl.when(owner != f)
        def _():
            copy = send(rows.at[panel, f], rows.at[panel, f], hs.at[slot], hr.at[place, f], (g, owner))
            if start:
                copy.start()
            else:
                copy.wait_send()

    def slots(t):
        if t == 0:
            return [(0, z)]
        if t == HALF:
            return [(2 * HALF - 1, (z + HALF) % NZ)]
        return [(2 * t - 1, (z - t + NZ) % NZ), (2 * t, (z + t) % NZ)]

    def ring_step(t):
        for sub in range(SUBS):
            for way in ways(t, sub):
                ring_got(t, way, sub)
                if t < HALF and way in ways(t + 1, sub):
                    begin(ring(t + 1, way, sub))
        for slot, panel in slots(t):
            hand(slot, panel, True)

    def col_send(panel, q, send_sem, recv_sem, peer):
        return send(cols.at[q, panel], cols.at[q, panel], send_sem, recv_sem, peer)

    def y_copies():
        return [
            col_send(a, f, ys.at[0], yr.at[0], (g_far, f2)),
            col_send(a, f, ys.at[1], yr.at[1], (g, f2)),
            col_send(a, f, ys.at[2], yr.at[2], (g_far, f)),
        ]

    y_items = [(a_far, f2), (a, f2), (a_far, f)]
    quad = [(0, f), (1, f2), (0, f2), (1, f)]

    def col_of(step, other):
        return ((x + step + NX) % NX) * 2 + (yh if other == 0 else 1 - yh)

    def x_copy(n, way):
        other, q = quad[n]
        return col_send(col_of(0, other), q, xs.at[way, n], xr.at[way, n], (at_x((1, -1)[way]), f))

    def x_got(n, way):
        other, q = quad[n]
        panel = col_of(-(1, -1)[way], other)
        col_send(panel, q, xs.at[way, n], xr.at[way, n], (at_x(0), f)).wait_recv()
        return panel, q

    forward = {(0, 0): 0, (0, 3): 1, (1, 1): 0, (1, 2): 1}

    def x_forward(n, way):
        other, q = quad[n]
        panel = col_of(-(1, -1)[way], other)
        return col_send(panel, q, fs.at[way, forward[way, n]], fr.at[way, forward[way, n]], (at_x((1, -1)[way]), f))

    def f_got(way, n):
        other, q = quad[n]
        panel = col_of(2, other)
        col_send(panel, q, fs.at[way, forward[way, n]], fr.at[way, forward[way, n]], (at_x(0), f)).wait_recv()
        return panel, q

    sibling = []

    def share(panel, q):
        n = len(sibling)
        sibling.append((panel, q))
        begin(col_send(panel, q, ss.at[n], sr.at[n], (g, f1)))

    def other_core(q):
        return q + 1 - 2 * core

    def share_got(n):
        panel, q = sibling[n]
        mine = other_core(q)
        col_send(panel, mine, ss.at[n], sr.at[n], (g, f1)).wait_recv()
        return panel, mine

    def base_table(q):
        kx = pack[q, 0:1, :]

        def step(i, carry):
            at = pl.ds(pl.multiple_of(i * 16, 16), 16)
            across = (lax.broadcasted_iota(jnp.int32, (16, width), 0) + i * 16) >> 1
            cos, sin = cos_sin(kx * (2 * across).astype(jnp.float32))
            base_c[q, at, :] = cos
            base_s[q, at, :] = sin
            return carry

        lax.fori_loop(0, PANEL // 16, step, 0)

    slope_count = PANEL * lax.axis_size("grid")
    group = a * NZ + f * 4
    turn_panels = [n * NZ + z for n in range(2 * NX)] + [group + n for n in range(4)]

    def turn_table(q):
        kx, ky = pack[q, 0:1, :], pack[q, 1:2, :]
        for n, panel in enumerate(turn_panels):
            upward = 2 * (panel % 64)
            star = panel * PANEL * NGS // slope_count
            for m in range(2):
                index = jnp.minimum(star + m, NGS - 1)
                turn_x = star_ref[index, 0].astype(jnp.float32)
                turn_y = (star_ref[index, 1] + upward).astype(jnp.float32)
                turn_p[2 * n + m : 2 * n + m + 1, :] = kx * turn_x + ky * turn_y
        weight = pack[q, 2:3, :]
        cos, sin = cos_sin(turn_p[...])
        turn_c[q] = cos * weight
        turn_s[q] = sin * weight

    def build(source, panel, q, turn, into):
        star = panel * PANEL * NGS // slope_count
        bound = ((star + 1) * slope_count + NGS - 1) // NGS - panel * PANEL
        c0, c1 = turn_c[q, pl.ds(2 * turn, 1), :], turn_c[q, pl.ds(2 * turn + 1, 1), :]
        s0, s1 = turn_s[q, pl.ds(2 * turn, 1), :], turn_s[q, pl.ds(2 * turn + 1, 1), :]

        def step(i, carry):
            at = pl.ds(pl.multiple_of(i * 16, 16), 16)
            first = lax.broadcasted_iota(jnp.int32, (16, width), 0) + i * 16 < bound
            tc, ts = jnp.where(first, c0, c1), jnp.where(first, s0, s1)
            value = source[at, :].astype(jnp.float32)
            bc, bs = base_c[q, at, :], base_s[q, at, :]
            into(i, (value * (bc * tc - bs * ts)).astype(jnp.bfloat16), (value * (bs * tc + bc * ts)).astype(jnp.bfloat16))
            return carry

        lax.fori_loop(0, PANEL // 16, step, 0)

    def build_col(item):
        panel, q = item
        half, part = q // 2, q % 2

        def into(i, cos, sin):
            at = pl.ds(pl.multiple_of(panel * PANEL + i * 16, 16), 16)
            cop[half, at, pl.ds(pl.multiple_of(part * 2 * width, 128), width)] = cos
            cop[half, at, pl.ds(pl.multiple_of(part * 2 * width + width, 128), width)] = sin

        build(cols.at[q, panel], panel * NZ + z, q, panel, into)

    for sub in range(SUBS):
        for way in (0, 1):
            begin(ring(1, way, sub))
    packs = [
        send(pack.at[f], pack.at[f], ps.at[n], pr.at[n], (g, peer)) for n, peer in enumerate((f1, f2, f3))
    ]
    for copy in packs:
        begin(copy)
    for copy in y_copies():
        begin(copy)
    for way in (0, 1):
        begin(x_copy(0, way))
    hand(0, z, True)
    share(a, f)

    base_table(f)
    turn_table(f)
    for n, q in enumerate((f1, f2, f3)):
        send(pack.at[q], pack.at[q], ps.at[n], pr.at[n], (g, q)).wait_recv()
        if n == 0:
            base_table(q)
            turn_table(q)

    ring_step(1)
    base_table(f2)
    turn_table(f2)
    base_table(f3)
    turn_table(f3)

    ring_step(2)
    for n, (panel, q) in enumerate(y_items):
        col_send(panel, q, ys.at[n], yr.at[n], (g, f)).wait_recv()
        for way in (0, 1):
            begin(x_copy(n + 1, way))
        share(panel, q)
    for way in (0, 1):
        item = x_got(0, way)
        if (way, 0) in forward:
            begin(x_forward(0, way))
        share(*item)
    build_col((a, f))
    build_col(share_got(0))

    ring_step(3)
    for n in range(3):
        build_col(y_items[n])
        build_col(share_got(1 + n))

    ring_step(4)
    build_col(sibling[4])
    build_col(sibling[5])
    build_col(share_got(4))
    build_col(share_got(5))

    ring_step(5)
    for way in (0, 1):
        item = x_got(1, way)
        if (way, 1) in forward:
            begin(x_forward(1, way))
        share(*item)
        build_col(item)
    ring_step(6)
    build_col(share_got(6))
    build_col(share_got(7))
    for n in (2, 3):
        for way in (0, 1):
            item = x_got(n, way)
            if (way, n) in forward:
                begin(x_forward(n, way))
            share(*item)
    build_col(sibling[8])
    build_col(sibling[9])

    ring_step(7)
    build_col(sibling[10])
    build_col(sibling[11])
    for n in range(8, 12):
        build_col(share_got(n))

    ring_step(8)
    for way, n in ((0, 0), (1, 1), (1, 2), (0, 3)):
        item = f_got(way, n)
        share(*item)
        build_col(item)
    for n in range(12, 16):
        build_col(share_got(n))

    ahead = (4 * f + 1 - z + NZ) % NZ < HALF

    def unit(n):
        place = jnp.where(ahead, n, 3 - n)
        panel = 4 * f + place
        for near in (True, False):
            half = yl if near else 1 - yl
            for q in ((f1,) if near else (f2, f3)):
                part = rows.at[panel, q]
                send(part, part, hs.at[0], hr.at[place, q], (g, f1)).wait_recv()
            for part in range(2):
                q = half * 2 + part

                def into(i, cos, sin, part=part):
                    at = pl.ds(pl.multiple_of(i * 16, 16), 16)
                    rop[at, 2 * part * width : (2 * part + 1) * width] = cos
                    rop[at, (2 * part + 1) * width : (2 * part + 2) * width] = sin

                build(rows.at[panel, q], a * NZ + panel, q, 2 * NX + place, into)

            def dot(i, carry):
                at = pl.ds(pl.multiple_of(i * 256, 256), 256)
                value = lax.dot_general(
                    rop[...], cop[half, at, :], (((1,), (1,)), ((), ())), preferred_element_type=jnp.float32
                )
                if near:
                    acc[:, at] = value
                else:
                    to = pl.ds(pl.multiple_of(place * PANEL, PANEL), PANEL)
                    out_ref[0, to, at] = (acc[:, at] + value).astype(jnp.bfloat16)
                return carry

            lax.fori_loop(0, cop.shape[1] // 256, dot, 0)

    lax.fori_loop(0, 4, lambda n, carry: (unit(n), carry)[1], 0)

    for copy in started:
        copy.wait_send()
    for t in range(HALF + 1):
        for slot, panel in slots(t):
            hand(slot, panel, False)


def on_device(amplitude, spectrum, freq_index, star_offsets, valid_mask):
    width = amplitude.shape[1]
    vmem = pl.BlockSpec(memory_space=pltpu.VMEM)
    dma = pltpu.SemaphoreType.DMA
    return pl.pallas_call(
        kernel,
        out_shape=jax.ShapeDtypeStruct((1, 4 * PANEL, 2 * NX * PANEL), jnp.bfloat16),
        in_specs=[vmem, vmem, vmem, pl.BlockSpec(memory_space=pltpu.SMEM), vmem],
        out_specs=vmem,
        scratch_shapes=[
            pltpu.VMEM((NZ, 4, PANEL, width), jnp.bfloat16),
            pltpu.VMEM((4, 2 * NX, PANEL, width), jnp.bfloat16),
            pltpu.VMEM((PANEL, 4 * width), jnp.bfloat16),
            pltpu.VMEM((2, 2 * NX * PANEL, 4 * width), jnp.bfloat16),
            pltpu.VMEM((4, 8, width), jnp.float32),
            pltpu.VMEM((4, PANEL, width), jnp.float32),
            pltpu.VMEM((4, PANEL, width), jnp.float32),
            pltpu.VMEM((24, width), jnp.float32),
            pltpu.VMEM((4, 24, width), jnp.float32),
            pltpu.VMEM((4, 24, width), jnp.float32),
            pltpu.VMEM((PANEL, PANEL), jnp.float32),
            pltpu.VMEM((PANEL, 2 * NX * PANEL), jnp.float32),
            dma((2, HALF, SUBS)), dma((2, HALF, SUBS)),
            dma((16,)), dma((4, 4)),
            dma((3,)), dma((3,)),
            dma((3,)), dma((3,)),
            dma((2, 4)), dma((2, 4)),
            dma((2, 2)), dma((2, 2)),
            dma((16,)), dma((16,)),
        ],
        compiler_params=pltpu.CompilerParams(
            collective_id=0, has_side_effects=True, vmem_limit_bytes=56 * 2**20
        ),
        cost_estimate=pl.CostEstimate(flops=2 * 512 * 1024 * 4096, bytes_accessed=2 * 2**20, transcendentals=0),
    )(amplitude, spectrum.reshape(1, width), freq_index, star_offsets, valid_mask.reshape(1, PANEL))


def solution(mesh):
    placed = (P("grid", "freq"), P("freq"), P(None, "freq"), P(), P("grid"))
    return jax.shard_map(
        on_device, mesh=mesh, in_specs=placed, out_specs=P("grid", "freq", None), check_vma=False
    )
```

time: 459 us -> 70.2 us (0.15)
  waiting for transfers between devices: 292 us -> 0 us
  starting transfers between devices: 135 us -> 0 us
  Pallas kernels: 0 us -> 66.4 us
  between operations: 13.7 us -> 0.01 us
  matrix products: 10.1 us -> 0 us
  other arithmetic: 7.28 us -> 0 us
    ppermute x7 -> x0, waiting for transfers between devices: 245 us -> none  [swapped(): lax.ppermute(array, axis, [(i, i ^ 1 << distance) for i in range(lax.axis...]
    ppermute x7 -> x0, starting transfers between devices: 135 us -> none  [swapped(): lax.ppermute(array, axis, [(i, i ^ 1 << distance) for i in range(lax.axis...]
    pallas_call x0 -> x1, Pallas kernels: none -> 66.4 us  [on_device(): pl.pallas_call(kernel, out_shape=jax.ShapeDtypeStruct((1, 4 * PANEL, 2 *...]
    reduce_scatter x1 -> x0, waiting for transfers between devices: 47 us -> none  [on_device(): lax.psum_scatter(lax.dot_general(row_block, column_block, (((1,), (1,)),...]
    dot_general x1 -> x0, matrix products: 10.1 us -> none  [on_device(): lax.dot_general(row_block, column_block, (((1,), (1,)), ((), ())), prefer...]
  transfers between devices with their start and end apart: 8 -> 0, of which waited for: 8 -> 0; matrix products, arithmetic and copies ran while one was open for 0% -> 0% of each run, Pallas kernels for 0% -> 0%
where the time goes in v1:
time: 70.2 us; the launch traced here: 70 us
  Pallas kernels  66.4 us (95%)
  local copies, waits for them, and re-layouts  3.63 us (5%)
    pallas_call x1, Pallas kernels, on_device(): pl.pallas_call(kernel, out_shape=jax.ShapeDtypeStruct((1, 4 * PANEL, 2 *...  66.4 us
    unnamed x4, local copies, waits for them, and re-layouts  3.63 us

profile of v1, /device:TPU:1, one launch (start us, length us, event | category | flops | bytes accessed | tf_op | source)
XLA Modules:
  0.0 70.0 jit_solution(6939664429644241170)
XLA Ops:
  0.0 0.0 copy-start
  0.0 0.7 copy-done
  0.7 0.7 copy.6.star_ref
  1.4 66.4 %shard_map.55 = bf16[1,512,1024]{2,1,0:T(8,128)(2,1)} custom-call(bf16[128,512]{1,0:T(8,128)(2,1)} %amp_ref.1, f32[1,512]{1,0:T(1,128)} %bitcast.2, s32[2,512]{1,0:T(2,128)} %freq_ref.1, s32[9,2]{1,0:T(8,128)} %copy.6.star_ref, s32[1,128]{1,0:T(1,128)} %bitcast.3), custom_call_target="tpu_custom_call" | custom-call | flops 4294967296 | bytes 2097152 | tf_op jit(solution)/shard_map/pallas_call | solution.py:381
  67.8 2.3 %copy.8 = bf16[1,512,1024]{2,1,0:T(8,128)(2,1)} copy(bf16[1,512,1024]{2,1,0:T(8,128)(2,1)} %shard_map.55) | data formatting | bytes 2097152
Async XLA Ops:
  0.0 0.7 copy-start

commit v2 on v1

--- a/solution.py
+++ b/solution.py
@@ -208,8 +208,8 @@
             star = panel * PANEL * NGS // slope_count
             for m in range(2):
                 index = jnp.minimum(star + m, NGS - 1)
-                turn_x = star_ref[index, 0].astype(jnp.float32)
-                turn_y = (star_ref[index, 1] + upward).astype(jnp.float32)
+                turn_x = star_ref[0, index].astype(jnp.float32)
+                turn_y = (star_ref[1, index] + upward).astype(jnp.float32)
                 turn_p[2 * n + m : 2 * n + m + 1, :] = kx * turn_x + ky * turn_y
         weight = pack[q, 2:3, :]
         cos, sin = cos_sin(turn_p[...])
@@ -231,7 +231,7 @@
             into(i, (value * (bc * tc - bs * ts)).astype(jnp.bfloat16), (value * (bs * tc + bc * ts)).astype(jnp.bfloat16))
             return carry
 
-        lax.fori_loop(0, PANEL // 16, step, 0)
+        lax.fori_loop(0, PANEL // 16, step, 0, unroll=8)
 
     def build_col(item):
         panel, q = item
@@ -243,6 +243,55 @@
             cop[half, at, pl.ds(pl.multiple_of(part * 2 * width + width, 128), width)] = sin
 
         build(cols.at[q, panel], panel * NZ + z, q, panel, into)
+
+    ahead = (4 * f + 1 - z + NZ) % NZ < HALF
+
+    def row_operand(place, q):
+        panel = 4 * f + place
+        part = q % 2
+
+        def into(i, cos, sin):
+            at = pl.ds(pl.multiple_of(place * PANEL + i * 16, 16), 16)
+            rop[q // 2, at, pl.ds(pl.multiple_of(part * 2 * width, 128), width)] = cos
+            rop[q // 2, at, pl.ds(pl.multiple_of(part * 2 * width + width, 128), width)] = sin
+
+        build(rows.at[panel, q], a * NZ + panel, q, 2 * NX + place, into)
+
+    def handed(place, q):
+        part = rows.at[4 * f + place, q]
+        send(part, part, hs.at[0], hr.at[place, q], (g, f1)).wait_recv()
+        row_operand(place, q)
+
+    def own_rows(t, of_core):
+        for _, panel in slots(t):
+            @pl.when(panel // 4 == f)
+            def _():
+                if of_core:
+                    row_operand(panel % 4, f)
+                else:
+                    handed(panel % 4, f1)
+
+    def product(m, near):
+        half = yl if near else 1 - yl
+        at = pl.ds(pl.multiple_of(jnp.where(ahead, 2 * m, 2 - 2 * m) * PANEL, PANEL), 2 * PANEL)
+
+        def dot(i, carry):
+            to = pl.ds(pl.multiple_of(i * 512, 512), 512)
+            value = lax.dot_general(
+                rop[half, at, :], cop[half, to, :], (((1,), (1,)), ((), ())), preferred_element_type=jnp.float32
+            )
+            if near:
+                acc[at, to] = value
+            else:
+                out_ref[0, at, to] = (acc[at, to] + value).astype(jnp.bfloat16)
+            return carry
+
+        lax.fori_loop(0, cop.shape[1] // 512, dot, 0)
+
+    def far_rows(m):
+        for n in range(2):
+            for q in (f2, f3):
+                handed(jnp.where(ahead, 2 * m + n, 3 - 2 * m - n), q)
 
     for sub in range(SUBS):
         for way in (0, 1):
@@ -267,11 +316,14 @@
             base_table(q)
             turn_table(q)
 
+    own_rows(0, True)
     ring_step(1)
     base_table(f2)
     turn_table(f2)
     base_table(f3)
     turn_table(f3)
+    own_rows(0, False)
+    own_rows(1, True)
 
     ring_step(2)
     for n, (panel, q) in enumerate(y_items):
@@ -286,86 +338,67 @@
         share(*item)
     build_col((a, f))
     build_col(share_got(0))
+    own_rows(1, False)
+    own_rows(2, True)
 
     ring_step(3)
     for n in range(3):
         build_col(y_items[n])
         build_col(share_got(1 + n))
+    own_rows(2, False)
+    own_rows(3, True)
 
     ring_step(4)
-    build_col(sibling[4])
-    build_col(sibling[5])
-    build_col(share_got(4))
-    build_col(share_got(5))
-
-    ring_step(5)
     for way in (0, 1):
         item = x_got(1, way)
         if (way, 1) in forward:
             begin(x_forward(1, way))
         share(*item)
-        build_col(item)
-    ring_step(6)
-    build_col(share_got(6))
-    build_col(share_got(7))
+    for n in (4, 5):
+        build_col(sibling[n])
+        build_col(share_got(n))
+    own_rows(3, False)
+    own_rows(4, True)
+
+    ring_step(5)
     for n in (2, 3):
         for way in (0, 1):
             item = x_got(n, way)
             if (way, n) in forward:
                 begin(x_forward(n, way))
             share(*item)
-    build_col(sibling[8])
-    build_col(sibling[9])
+    for n in (6, 7):
+        build_col(sibling[n])
+        build_col(share_got(n))
+    own_rows(4, False)
+    own_rows(5, True)
+
+    ring_step(6)
+    for n in range(8, 12):
+        build_col(sibling[n])
+        build_col(share_got(n))
+    own_rows(5, False)
+    own_rows(6, True)
 
     ring_step(7)
-    build_col(sibling[10])
-    build_col(sibling[11])
-    for n in range(8, 12):
+    for way, n in ((0, 0), (1, 1), (1, 2), (0, 3)):
+        share(*f_got(way, n))
+    own_rows(6, False)
+    own_rows(7, True)
+    for n in range(12, 16):
+        build_col(sibling[n])
         build_col(share_got(n))
+    own_rows(7, False)
+    product(0, True)
 
     ring_step(8)
-    for way, n in ((0, 0), (1, 1), (1, 2), (0, 3)):
-        item = f_got(way, n)
-        share(*item)
-        build_col(item)
-    for n in range(12, 16):
-        build_col(share_got(n))
-
-    ahead = (4 * f + 1 - z + NZ) % NZ < HALF
-
-    def unit(n):
-        place = jnp.where(ahead, n, 3 - n)
-        panel = 4 * f + place
-        for near in (True, False):
-            half = yl if near else 1 - yl
-            for q in ((f1,) if near else (f2, f3)):
-                part = rows.at[panel, q]
-                send(part, part, hs.at[0], hr.at[place, q], (g, f1)).wait_recv()
-            for part in range(2):
-                q = half * 2 + part
-
-                def into(i, cos, sin, part=part):
-                    at = pl.ds(pl.multiple_of(i * 16, 16), 16)
-                    rop[at, 2 * part * width : (2 * part + 1) * width] = cos
-                    rop[at, (2 * part + 1) * width : (2 * part + 2) * width] = sin
-
-                build(rows.at[panel, q], a * NZ + panel, q, 2 * NX + place, into)
-
-            def dot(i, carry):
-                at = pl.ds(pl.multiple_of(i * 256, 256), 256)
-                value = lax.dot_general(
-                    rop[...], cop[half, at, :], (((1,), (1,)), ((), ())), preferred_element_type=jnp.float32
-                )
-                if near:
-                    acc[:, at] = value
-                else:
-                    to = pl.ds(pl.multiple_of(place * PANEL, PANEL), PANEL)
-                    out_ref[0, to, at] = (acc[:, at] + value).astype(jnp.bfloat16)
-                return carry
-
-            lax.fori_loop(0, cop.shape[1] // 256, dot, 0)
-
-    lax.fori_loop(0, 4, lambda n, carry: (unit(n), carry)[1], 0)
+    own_rows(8, True)
+    far_rows(0)
+    product(0, False)
+    own_rows(8, False)
+    product(1, True)
+    far_rows(1)
+    product(1, False)
 
     for copy in started:
         copy.wait_send()
@@ -386,7 +419,7 @@
         scratch_shapes=[
             pltpu.VMEM((NZ, 4, PANEL, width), jnp.bfloat16),
             pltpu.VMEM((4, 2 * NX, PANEL, width), jnp.bfloat16),
-            pltpu.VMEM((PANEL, 4 * width), jnp.bfloat16),
+            pltpu.VMEM((2, 4 * PANEL, 4 * width), jnp.bfloat16),
             pltpu.VMEM((2, 2 * NX * PANEL, 4 * width), jnp.bfloat16),
             pltpu.VMEM((4, 8, width), jnp.float32),
             pltpu.VMEM((4, PANEL, width), jnp.float32),
@@ -395,7 +428,7 @@
             pltpu.VMEM((4, 24, width), jnp.float32),
             pltpu.VMEM((4, 24, width), jnp.float32),
             pltpu.VMEM((PANEL, PANEL), jnp.float32),
-            pltpu.VMEM((PANEL, 2 * NX * PANEL), jnp.float32),
+            pltpu.VMEM((4 * PANEL, 2 * NX * PANEL), jnp.float32),
             dma((2, HALF, SUBS)), dma((2, HALF, SUBS)),
             dma((16,)), dma((4, 4)),
             dma((3,)), dma((3,)),
@@ -405,10 +438,10 @@
             dma((16,)), dma((16,)),
         ],
         compiler_params=pltpu.CompilerParams(
-            collective_id=0, has_side_effects=True, vmem_limit_bytes=56 * 2**20
+            collective_id=0, has_side_effects=True, vmem_limit_bytes=36 * 2**20
         ),
         cost_estimate=pl.CostEstimate(flops=2 * 512 * 1024 * 4096, bytes_accessed=2 * 2**20, transcendentals=0),
-    )(amplitude, spectrum.reshape(1, width), freq_index, star_offsets, valid_mask.reshape(1, PANEL))
+    )(amplitude, spectrum.reshape(1, width), freq_index, star_offsets.T, valid_mask.reshape(1, PANEL))
 
 
 def solution(mesh):

time: 70.2 us -> 56 us (0.80)
  Pallas kernels: 66.4 us -> 52.3 us
    pallas_call x1, Pallas kernels: 66.4 us -> 52.3 us  [on_device(): pl.pallas_call(kernel, out_shape=jax.ShapeDtypeStruct((1, 4 * PANEL, 2 *...]
    unnamed x4 -> x11, local copies, waits for them, and re-layouts: 3.63 us -> 3.25 us
where the time goes in v2:
time: 56 us; the launch traced here: 55.5 us
  Pallas kernels  52.3 us (93%)
  local copies, waits for them, and re-layouts  3.25 us (6%)
    pallas_call x1, Pallas kernels, on_device(): pl.pallas_call(kernel, out_shape=jax.ShapeDtypeStruct((1, 4 * PANEL, 2 *...  52.3 us
    unnamed x11, local copies, waits for them, and re-layouts  3.25 us

profile of v2, /device:TPU:1, one launch (start us, length us, event | category | flops | bytes accessed | tf_op | source)
XLA Modules:
  0.0 55.5 jit_solution(5451948510151754544)
XLA Ops:
  0.0 0.0 copy-start.1
  0.0 0.0 copy-start.3
  0.0 0.0 copy-start.4
  0.0 0.7 %copy-done.1 = s32[2,512]{1,0:T(2,128)S(1)} copy-done((s32[2,512]{1,0:T(2,128)S(1)}, s32[2,512]{1,0:T(2,128)}, u32[]{:S(2)}) %copy-start.1) | copy-done | bytes 4120
  0.7 0.0 copy-done.3
  0.7 0.0 copy-done.4
  0.7 0.0 copy-start
  0.7 0.9 %copy-done = bf16[128,512]{1,0:T(8,128)(2,1)S(1)} copy-done((bf16[128,512]{1,0:T(8,128)(2,1)S(1)}, bf16[128,512]{1,0:T(8,128)(2,1)}, u32[]{:S(2)}) %copy-start) | copy-done | bytes 131096
  1.6 0.0 copy-start.2
  1.6 0.7 %copy-done.2 = f32[512]{0:T(512)S(1)} copy-done((f32[512]{0:T(512)S(1)}, f32[512]{0:T(512)}, u32[]{:S(2)}) %copy-start.2) | copy-done | bytes 2072
  2.3 52.3 %shard_map.55 = bf16[1,512,1024]{2,1,0:T(8,128)(2,1)S(1)} custom-call(bf16[128,512]{1,0:T(8,128)(2,1)S(1)} %copy-done, f32[1,512]{1,0:T(1,128)S(1)} %bitcast.3, s32[2,512]{1,0:T(2,128)S(1)} %copy-done.1, s32[2,9]{1,0:T(2,128)S(1)} %bitcast.4, s32[1,128]{1,0:T(1,128)S(1)} %bitcast.5), custom_call_target="tpu_custom_call" | custom-call | flops 4294967296 | bytes 2097152 | tf_op jit(solution)/shard_map/pallas_call | solution.py:414
  54.6 1.0 %copy.7 = bf16[1,512,1024]{2,1,0:T(8,128)(2,1)} copy(bf16[1,512,1024]{2,1,0:T(8,128)(2,1)S(1)} %shard_map.55) | data formatting | bytes 2097152
Async XLA Ops:
  0.0 0.7 %copy-start.1 = (s32[2,512]{1,0:T(2,128)S(1)}, s32[2,512]{1,0:T(2,128)}, u32[]{:S(2)}) copy-start(s32[2,512]{1,0:T(2,128)} %freq_ref.1) | copy-start | bytes 12292
  0.0 0.7 %copy-start.3 = (s32[9,2]{0,1:T(2,128)S(1)}, s32[9,2]{0,1:T(2,128)}, u32[]{:S(2)}) copy-start(s32[9,2]{0,1:T(2,128)} %param.8) | copy-start | bytes 220
  0.0 0.7 %copy-start.4 = (s32[128]{0:T(128)S(1)}, s32[128]{0:T(128)}, u32[]{:S(2)}) copy-start(s32[128]{0:T(128)} %param.9) | copy-start | bytes 1540
  0.7 0.9 %copy-start = (bf16[128,512]{1,0:T(8,128)(2,1)S(1)}, bf16[128,512]{1,0:T(8,128)(2,1)}, u32[]{:S(2)}) copy-start(bf16[128,512]{1,0:T(8,128)(2,1)} %amp_ref.1) | copy-start | bytes 393220
  1.6 0.7 %copy-start.2 = (f32[512]{0:T(512)S(1)}, f32[512]{0:T(512)}, u32[]{:S(2)}) copy-start(f32[512]{0:T(512)} %param.6) | copy-start | bytes 6148

commit v3 on v2

--- a/solution.py
+++ b/solution.py
@@ -276,7 +276,7 @@
         at = pl.ds(pl.multiple_of(jnp.where(ahead, 2 * m, 2 - 2 * m) * PANEL, PANEL), 2 * PANEL)
 
         def dot(i, carry):
-            to = pl.ds(pl.multiple_of(i * 512, 512), 512)
+            to = pl.ds(pl.multiple_of(i * 1024, 1024), 1024)
             value = lax.dot_general(
                 rop[half, at, :], cop[half, to, :], (((1,), (1,)), ((), ())), preferred_element_type=jnp.float32
             )
@@ -286,7 +286,7 @@
                 out_ref[0, at, to] = (acc[at, to] + value).astype(jnp.bfloat16)
             return carry
 
-        lax.fori_loop(0, cop.shape[1] // 512, dot, 0)
+        lax.fori_loop(0, cop.shape[1] // 1024, dot, 0)
 
     def far_rows(m):
         for n in range(2):
@@ -317,6 +317,25 @@
             turn_table(q)
 
     own_rows(0, True)
+    def y_step(n):
+        panel, q = y_items[n]
+        col_send(panel, q, ys.at[n], yr.at[n], (g, f)).wait_recv()
+        for way in (0, 1):
+            begin(x_copy(n + 1, way))
+        share(panel, q)
+
+    def x_step(n):
+        for way in (0, 1):
+            item = x_got(n, way)
+            if (way, n) in forward:
+                begin(x_forward(n, way))
+            share(*item)
+
+    def both_cols(*numbers):
+        for n in numbers:
+            build_col(sibling[n])
+            build_col(share_got(n))
+
     ring_step(1)
     base_table(f2)
     turn_table(f2)
@@ -324,79 +343,57 @@
     turn_table(f3)
     own_rows(0, False)
     own_rows(1, True)
+    y_step(0)
+    y_step(1)
 
     ring_step(2)
-    for n, (panel, q) in enumerate(y_items):
-        col_send(panel, q, ys.at[n], yr.at[n], (g, f)).wait_recv()
-        for way in (0, 1):
-            begin(x_copy(n + 1, way))
-        share(panel, q)
-    for way in (0, 1):
-        item = x_got(0, way)
-        if (way, 0) in forward:
-            begin(x_forward(0, way))
-        share(*item)
-    build_col((a, f))
-    build_col(share_got(0))
+    y_step(2)
+    x_step(0)
+    both_cols(0)
     own_rows(1, False)
     own_rows(2, True)
 
     ring_step(3)
-    for n in range(3):
-        build_col(y_items[n])
-        build_col(share_got(1 + n))
+    both_cols(1, 2, 3)
     own_rows(2, False)
     own_rows(3, True)
+    x_step(1)
 
     ring_step(4)
-    for way in (0, 1):
-        item = x_got(1, way)
-        if (way, 1) in forward:
-            begin(x_forward(1, way))
-        share(*item)
-    for n in (4, 5):
-        build_col(sibling[n])
-        build_col(share_got(n))
+    x_step(2)
+    both_cols(4, 5)
     own_rows(3, False)
     own_rows(4, True)
 
     ring_step(5)
-    for n in (2, 3):
-        for way in (0, 1):
-            item = x_got(n, way)
-            if (way, n) in forward:
-                begin(x_forward(n, way))
-            share(*item)
-    for n in (6, 7):
-        build_col(sibling[n])
-        build_col(share_got(n))
+    x_step(3)
+    share(*f_got(0, 0))
+    both_cols(6, 7, 8, 9)
     own_rows(4, False)
     own_rows(5, True)
 
     ring_step(6)
-    for n in range(8, 12):
-        build_col(sibling[n])
-        build_col(share_got(n))
+    share(*f_got(1, 1))
+    share(*f_got(1, 2))
+    both_cols(10, 11, 12)
     own_rows(5, False)
     own_rows(6, True)
+    both_cols(13)
 
     ring_step(7)
-    for way, n in ((0, 0), (1, 1), (1, 2), (0, 3)):
-        share(*f_got(way, n))
+    share(*f_got(0, 3))
     own_rows(6, False)
     own_rows(7, True)
-    for n in range(12, 16):
-        build_col(sibling[n])
-        build_col(share_got(n))
+    both_cols(14, 15)
     own_rows(7, False)
     product(0, True)
 
     ring_step(8)
     own_rows(8, True)
+    own_rows(8, False)
+    product(1, True)
     far_rows(0)
     product(0, False)
-    own_rows(8, False)
-    product(1, True)
     far_rows(1)
     product(1, False)
 

time: 56 us -> 54.3 us (0.970)
  Pallas kernels: 52.3 us -> 50.3 us
    pallas_call x1, Pallas kernels: 52.3 us -> 50.3 us  [on_device(): pl.pallas_call(kernel, out_shape=jax.ShapeDtypeStruct((1, 4 * PANEL, 2 *...]
where the time goes in v3:
time: 54.3 us; the launch traced here: 53.6 us
  Pallas kernels  50.3 us (93%)
  local copies, waits for them, and re-layouts  3.25 us (6%)
    pallas_call x1, Pallas kernels, on_device(): pl.pallas_call(kernel, out_shape=jax.ShapeDtypeStruct((1, 4 * PANEL, 2 *...  50.3 us
    unnamed x11, local copies, waits for them, and re-layouts  3.25 us

profile of v3, /device:TPU:1, one launch (start us, length us, event | category | flops | bytes accessed | tf_op | source)
XLA Modules:
  0.0 53.6 jit_solution(10402901208634187387)
XLA Ops:
  0.0 0.0 copy-start.1
  0.0 0.0 copy-start.3
  0.0 0.0 copy-start.4
  0.0 0.7 %copy-done.1 = s32[2,512]{1,0:T(2,128)S(1)} copy-done((s32[2,512]{1,0:T(2,128)S(1)}, s32[2,512]{1,0:T(2,128)}, u32[]{:S(2)}) %copy-start.1) | copy-done | bytes 4120
  0.7 0.0 copy-done.3
  0.7 0.0 copy-done.4
  0.7 0.0 copy-start
  0.7 0.9 %copy-done = bf16[128,512]{1,0:T(8,128)(2,1)S(1)} copy-done((bf16[128,512]{1,0:T(8,128)(2,1)S(1)}, bf16[128,512]{1,0:T(8,128)(2,1)}, u32[]{:S(2)}) %copy-start) | copy-done | bytes 131096
  1.6 0.0 copy-start.2
  1.6 0.7 %copy-done.2 = f32[512]{0:T(512)S(1)} copy-done((f32[512]{0:T(512)S(1)}, f32[512]{0:T(512)}, u32[]{:S(2)}) %copy-start.2) | copy-done | bytes 2072
  2.3 50.3 %shard_map.55 = bf16[1,512,1024]{2,1,0:T(8,128)(2,1)S(1)} custom-call(bf16[128,512]{1,0:T(8,128)(2,1)S(1)} %copy-done, f32[1,512]{1,0:T(1,128)S(1)} %bitcast.3, s32[2,512]{1,0:T(2,128)S(1)} %copy-done.1, s32[2,9]{1,0:T(2,128)S(1)} %bitcast.4, s32[1,128]{1,0:T(1,128)S(1)} %bitcast.5), custom_call_target="tpu_custom_call" | custom-call | flops 4294967296 | bytes 2097152 | tf_op jit(solution)/shard_map/pallas_call | solution.py:411
  52.6 1.0 %copy.7 = bf16[1,512,1024]{2,1,0:T(8,128)(2,1)} copy(bf16[1,512,1024]{2,1,0:T(8,128)(2,1)S(1)} %shard_map.55) | data formatting | bytes 2097152
Async XLA Ops:
  0.0 0.7 %copy-start.1 = (s32[2,512]{1,0:T(2,128)S(1)}, s32[2,512]{1,0:T(2,128)}, u32[]{:S(2)}) copy-start(s32[2,512]{1,0:T(2,128)} %freq_ref.1) | copy-start | bytes 12292
  0.0 0.7 %copy-start.3 = (s32[9,2]{0,1:T(2,128)S(1)}, s32[9,2]{0,1:T(2,128)}, u32[]{:S(2)}) copy-start(s32[9,2]{0,1:T(2,128)} %param.8) | copy-start | bytes 220
  0.0 0.7 %copy-start.4 = (s32[128]{0:T(128)S(1)}, s32[128]{0:T(128)}, u32[]{:S(2)}) copy-start(s32[128]{0:T(128)} %param.9) | copy-start | bytes 1540
  0.7 0.9 %copy-start = (bf16[128,512]{1,0:T(8,128)(2,1)S(1)}, bf16[128,512]{1,0:T(8,128)(2,1)}, u32[]{:S(2)}) copy-start(bf16[128,512]{1,0:T(8,128)(2,1)} %amp_ref.1) | copy-start | bytes 393220
  1.6 0.7 %copy-start.2 = (f32[512]{0:T(512)S(1)}, f32[512]{0:T(512)}, u32[]{:S(2)}) copy-start(f32[512]{0:T(512)} %param.6) | copy-start | bytes 6148

commit v4 on v3

--- a/solution.py
+++ b/solution.py
@@ -31,8 +31,8 @@
 
 
 def kernel(
-    amp_ref, spec_ref, freq_ref, star_ref, mask_ref, out_ref,
-    rows, cols, rop, cop, pack, base_c, base_s, turn_p, turn_c, turn_s, mask_t, acc,
+    amp_ref, spec_ref, freq_ref, star_ref, out_ref,
+    rows, cols, rop, cop, pack, base_c, base_s, turn_p, turn_c, turn_s, acc,
     zs, zr, hs, hr, ps, pr, ys, yr, xs, xr, fs, fr, ss, sr,
 ):
     g, f = lax.axis_index("grid"), lax.axis_index("freq")
@@ -61,12 +61,8 @@
     for peer in peers:
         pl.semaphore_signal(barrier, inc=1, device_id=peer, device_id_type=MESH)
 
-    mask_t[...] = jnp.broadcast_to(mask_ref[...].astype(jnp.float32), (PANEL, PANEL)).T
-    for n in range(width // 128):
-        lanes = pl.ds(n * 128, 128)
-        masked = (amp_ref[:, lanes].astype(jnp.float32) * mask_t[...]).astype(jnp.bfloat16)
-        rows[z, f, :, lanes] = masked
-        cols[f, a, :, lanes] = masked
+    rows[z, f] = amp_ref[...]
+    cols[f, a] = amp_ref[...]
     total = width * lax.axis_size("freq")
     pack[f, 0:2, :] = freq_ref[...].astype(jnp.float32)
     pack[f, 2:3, :] = jnp.sqrt(spec_ref[...] / total)
@@ -406,12 +402,13 @@
 
 def on_device(amplitude, spectrum, freq_index, star_offsets, valid_mask):
     width = amplitude.shape[1]
+    masked = amplitude * valid_mask.astype(jnp.bfloat16)[:, None]
     vmem = pl.BlockSpec(memory_space=pltpu.VMEM)
     dma = pltpu.SemaphoreType.DMA
     return pl.pallas_call(
         kernel,
         out_shape=jax.ShapeDtypeStruct((1, 4 * PANEL, 2 * NX * PANEL), jnp.bfloat16),
-        in_specs=[vmem, vmem, vmem, pl.BlockSpec(memory_space=pltpu.SMEM), vmem],
+        in_specs=[vmem, vmem, vmem, pl.BlockSpec(memory_space=pltpu.SMEM)],
         out_specs=vmem,
         scratch_shapes=[
             pltpu.VMEM((NZ, 4, PANEL, width), jnp.bfloat16),
@@ -424,7 +421,6 @@
             pltpu.VMEM((24, width), jnp.float32),
             pltpu.VMEM((4, 24, width), jnp.float32),
             pltpu.VMEM((4, 24, width), jnp.float32),
-            pltpu.VMEM((PANEL, PANEL), jnp.float32),
             pltpu.VMEM((4 * PANEL, 2 * NX * PANEL), jnp.float32),
             dma((2, HALF, SUBS)), dma((2, HALF, SUBS)),
             dma((16,)), dma((4, 4)),
@@ -438,7 +434,7 @@
             collective_id=0, has_side_effects=True, vmem_limit_bytes=36 * 2**20
         ),
         cost_estimate=pl.CostEstimate(flops=2 * 512 * 1024 * 4096, bytes_accessed=2 * 2**20, transcendentals=0),
-    )(amplitude, spectrum.reshape(1, width), freq_index, star_offsets.T, valid_mask.reshape(1, PANEL))
+    )(masked, spectrum.reshape(1, width), freq_index, star_offsets.T)
 
 
 def solution(mesh):

time: 54.3 us -> 53.7 us (0.989)
  local copies, waits for them, and re-layouts: 3.25 us -> 1.64 us
  other arithmetic: 0 us -> 1.03 us
    unnamed x11 -> x9, local copies, waits for them, and re-layouts: 3.25 us -> 1.64 us
    mul x0 -> x1, other arithmetic: none -> 1.02 us  [on_device(): masked = amplitude * valid_mask.astype(jnp.bfloat16)[:, None]]
where the time goes in v4:
time: 53.7 us; the launch traced here: 53 us
  Pallas kernels  50.3 us (94%)
  local copies, waits for them, and re-layouts  1.64 us (3%)
  other arithmetic  1.03 us (2%)
    pallas_call x1, Pallas kernels, on_device(): pl.pallas_call(kernel, out_shape=jax.ShapeDtypeStruct((1, 4 * PANEL, 2 *...  50.3 us
    unnamed x9, local copies, waits for them, and re-layouts  1.64 us

profile of v4, /device:TPU:1, one launch (start us, length us, event | category | flops | bytes accessed | tf_op | source)
XLA Modules:
  0.0 53.0 jit_solution(16674638976028145486)
XLA Ops:
  0.0 0.0 copy-start.3
  0.0 0.7 %copy-done.3 = s32[128]{0:T(128)S(1)} copy-done((s32[128]{0:T(128)S(1)}, s32[128]{0:T(128)}, u32[]{:S(2)}) %copy-start.3) | copy-done | bytes 536
  0.7 0.0 copy-start
  0.7 0.0 copy-start.1
  0.7 0.0 copy-start.2
  0.7 1.0 %broadcast_multiply_fusion.amp_ref = bf16[128,512]{1,0:T(8,128)(2,1)S(1)} fusion(bf16[128,512]{1,0:T(8,128)(2,1)} %param.5, bf16[128]{0:T(256)(128)(2,1)S(1)} %convert_element_type.3), kind=kLoop, calls=%fused_computation | loop fusion | flops 65536 | bytes 262400 | tf_op jit(solution)/shard_map/mul | solution.py:405
  1.7 0.0 copy-done
  1.7 0.0 copy-done.1
  1.7 0.0 copy-done.2
  1.7 50.3 %shard_map.55 = bf16[1,512,1024]{2,1,0:T(8,128)(2,1)S(1)} custom-call(bf16[128,512]{1,0:T(8,128)(2,1)S(1)} %broadcast_multiply_fusion.amp_ref, f32[1,512]{1,0:T(1,128)S(1)} %bitcast.2, s32[2,512]{1,0:T(2,128)S(1)} %copy-done, s32[2,9]{1,0:T(2,128)S(1)} %bitcast.3), custom_call_target="tpu_custom_call" | custom-call | flops 4294967296 | bytes 2097152 | tf_op jit(solution)/shard_map/pallas_call | solution.py:408
  52.0 1.0 %copy.7 = bf16[1,512,1024]{2,1,0:T(8,128)(2,1)} copy(bf16[1,512,1024]{2,1,0:T(8,128)(2,1)S(1)} %shard_map.55) | data formatting | bytes 2097152
  (1 shorter events, 0.0 us)
Async XLA Ops:
  0.0 0.7 %copy-start.3 = (s32[128]{0:T(128)S(1)}, s32[128]{0:T(128)}, u32[]{:S(2)}) copy-start(s32[128]{0:T(128)} %param.9) | copy-start | bytes 1540
  0.7 1.0 %copy-start = (s32[2,512]{1,0:T(2,128)S(1)}, s32[2,512]{1,0:T(2,128)}, u32[]{:S(2)}) copy-start(s32[2,512]{1,0:T(2,128)} %freq_ref.1) | copy-start | bytes 12292
  0.7 1.1 %copy-start.1 = (f32[512]{0:T(512)S(1)}, f32[512]{0:T(512)}, u32[]{:S(2)}) copy-start(f32[512]{0:T(512)} %param.6) | copy-start | bytes 6148
  0.7 1.1 %copy-start.2 = (s32[9,2]{0,1:T(2,128)S(1)}, s32[9,2]{0,1:T(2,128)}, u32[]{:S(2)}) copy-start(s32[9,2]{0,1:T(2,128)} %param.8) | copy-start | bytes 220
